TPU v7x, 32 devices: a whole 2x2x4 slice. The times are simulated.
32 devices in a mesh: groups: 2 (over y), rows: 4 (over z), cols: 4 (over x, core).
Axes of the slice: x: 2, y: 2, z: 4, core: 2. Of those that a mesh axis runs over, the one named last changes fastest.
Arguments:
- covariance: float32 [1024, 512], P(('groups', 'rows'), 'cols'), parts along dimension 0, as said below
- block_cols: int32 [8, 7], P(('groups', 'rows')), parts along dimension 0, may hold values from 0 to 3, as said below
- trans_blocks: float32 [8, 7, 128, 128], P(('groups', 'rows')), parts along dimension 0, may hold values from -0.1875 to 0.1875
- noise_pattern: int32 [8], P(('groups', 'rows')), parts along dimension 0, may hold values from 0 to 7
- noise_table: float32 [8, 128, 128], replicated, may hold values from -3 to 3
Outputs:
- forecast: float32 [1024, 512], P(('groups', 'rows'), 'cols'), parts along dimension 0
There are 2 independent parts, one for each index of `groups`. A program takes and returns all parts, laid end to end along the dimension named above; an argument that names none is the same for every part. Nothing has to cross between parts.
Inputs may be any that keep to these rules, and one draw needn't show every extreme that they name: covariance is exactly symmetric. block_cols[i, 0] = i; for k >= 1, block_cols[i, k] = (i + o) mod 4 for 6 distinct nonzero offsets o between -4 and 4.
All inputs are finite; a program needn't handle non-finite values.
Results may differ from a plain program's by a relative error of at most 0.000096.
Values sent between devices are 32-bit elements; how exact they have to be, the bound alone decides.
A program may use at most 64 MiB of HBM per device.

v0:
```python
import jax
import jax.numpy as jnp
from jax import lax
from jax.sharding import PartitionSpec as P

REACH = 4


def passed_along(value, axis, by):
    size = lax.axis_size(axis)
    return lax.ppermute(value, axis, [(i, (i + by) % size) for i in range(size)])


def neighbor_strips(local_tile, shards):
    lower_side = [None] * shards
    upper_side = [None] * shards
    for distance in list(range(-shards, 0)) + list(range(1, shards + 1)):
        incoming = passed_along(local_tile, "rows", -distance)
        if distance < 0:
            lower_side[shards + distance] = incoming
        else:
            upper_side[distance - 1] = incoming
    return (lower_side, upper_side)


def propagate_rows(local_tile, block_cols, trans_blocks):
    tile_height, tile_width = local_tile.shape
    blocks_here = block_cols.shape[0]
    block_size = trans_blocks.shape[2]
    total_blocks = blocks_here * lax.axis_size("rows")
    shards = -(-REACH // blocks_here)
    lower_side, upper_side = neighbor_strips(local_tile, shards)
    extended = jnp.concatenate(lower_side + [local_tile] + upper_side, axis=0)
    ext_blocks = extended.reshape(-1, block_size, tile_width)
    local_rows = jnp.arange(blocks_here, dtype=jnp.int32)
    first_block = lax.axis_index("rows") * blocks_here + local_rows
    offsets = (block_cols - first_block[:, None] + REACH) % total_blocks - REACH
    positions = shards * blocks_here + local_rows[:, None] + offsets
    result = jnp.zeros((blocks_here, block_size, tile_width), jnp.float32)
    for column_slot in range(block_cols.shape[1]):
        picked = jnp.take(ext_blocks, positions[:, column_slot], axis=0)
        result = result + jnp.einsum(
            "iab,ibw->iaw", trans_blocks[:, column_slot], picked, precision=lax.Precision.HIGHEST
        )
    return result.reshape(tile_height, tile_width)


def transpose_tile(local_tile):
    tile_height, tile_width = local_tile.shape
    col_count = lax.axis_size("cols")
    row_group = lax.axis_size("rows") // col_count
    quarter = tile_height // col_count
    section_one = lax.all_to_all(local_tile, "cols", split_axis=0, concat_axis=1, tiled=True)
    arrived = lax.all_to_all(
        lax.all_to_all(section_one, "rows", split_axis=1, concat_axis=0, tiled=True),
        "cols",
        split_axis=0,
        concat_axis=1,
        tiled=True,
    )
    pieces = arrived.reshape(row_group, quarter, col_count, tile_height)
    return jnp.transpose(pieces, (3, 0, 2, 1)).reshape(tile_height, tile_width)


def noise_tile(noise_pattern, noise_table, tile_height, tile_width):
    block_size = noise_table.shape[1]
    kinds = noise_table.shape[0]
    blocks_here = noise_pattern.shape[0]
    row_group = lax.axis_size("rows") // lax.axis_size("cols")
    row_index = lax.axis_index("rows")
    present = (row_index // row_group == lax.axis_index("cols")).astype(jnp.float32)
    symmetric = (noise_table + jnp.transpose(noise_table, (0, 2, 1))) * 0.5
    onehot = (noise_pattern[:, None] == jnp.arange(kinds, dtype=jnp.int32)[None, :]).astype(
        jnp.float32
    )
    picked = jnp.dot(
        onehot,
        symmetric.reshape(kinds, block_size * block_size),
        precision=lax.Precision.HIGHEST,
        preferred_element_type=jnp.float32,
    )
    picked = picked.reshape(blocks_here, block_size, block_size)
    identity = jnp.eye(blocks_here, dtype=jnp.float32)
    diagonal_tile = (picked[:, :, None, :] * identity[:, None, :, None]).reshape(
        tile_height, tile_height
    )
    start = row_index % row_group * tile_height
    placed = lax.dynamic_update_slice(
        jnp.zeros((tile_height, tile_width), jnp.float32), diagonal_tile, (jnp.int32(0), start)
    )
    return present * placed


def body(covariance, block_cols, trans_blocks, noise_pattern, noise_table):
    tile_height, tile_width = covariance.shape
    propagated = propagate_rows(covariance, block_cols, trans_blocks)
    carried = propagate_rows(transpose_tile(propagated), block_cols, trans_blocks)
    return carried + noise_tile(noise_pattern, noise_table, tile_height, tile_width)


def solution(mesh):
    placed = (
        P(("groups", "rows"), "cols"),
        P(("groups", "rows"), None),
        P(("groups", "rows"), None, None, None),
        P(("groups", "rows")),
        P(),
    )
    return jax.shard_map(
        body, mesh=mesh, in_specs=placed, out_specs=P(("groups", "rows"), "cols"), check_vma=False
    )
```

profile of v0, /device:TPU:0, one launch (start us, length us, event | category | flops | bytes accessed | tf_op | source)
XLA Modules:
  0.0 61.3 jit_solution(10600114747214594998)
XLA Ops:
  0.0 0.8 %collective-permute-start = (f32[128,128]{1,0:T(8,128)}, f32[128,128]{1,0:T(8,128)S(1)}, u32[]{:S(2)}, u32[]{:S(2)}) collective-permute-start(f32[128,128]{1,0:T(8,128)} %param.7), channel_id=1, source_target_pairs={{0,0},{4,4},{8,8},{12,12},{1,1},{5,5},{9,9},{13,13},{2,2},{6,6},{1... | collective-permute-start | bytes 196616 | tf_op jit(solution)/shard_map/ppermute | solution.py:11
  0.8 5.0 %collective-permute-start.1 = (f32[128,128]{1,0:T(8,128)}, f32[128,128]{1,0:T(8,128)S(1)}, u32[]{:S(2)}, u32[]{:S(2)}) collective-permute-start(f32[128,128]{1,0:T(8,128)} %param.7), channel_id=1, source_target_pairs={{0,12},{4,0},{8,4},{12,8},{1,13},{5,1},{9,5},{13,9},{2,14},{6,2},{... | collective-permute-start | bytes 196616 | tf_op jit(solution)/shard_map/ppermute | solution.py:11
  5.9 1.0 %collective-permute-start.3 = (f32[128,128]{1,0:T(8,128)}, f32[128,128]{1,0:T(8,128)S(1)}, u32[]{:S(2)}, u32[]{:S(2)}) collective-permute-start(f32[128,128]{1,0:T(8,128)} %param.7), channel_id=1, source_target_pairs={{0,4},{4,8},{8,12},{12,0},{1,5},{5,9},{9,13},{13,1},{2,6},{6,10},{... | collective-permute-start | bytes 196616 | tf_op jit(solution)/shard_map/ppermute | solution.py:11
  6.9 0.7 %copy-done.3 = s32[1,7]{1,0:T(1,128)S(1)} copy-done((s32[1,7]{1,0:T(1,128)S(1)}, s32[1,7]{1,0:T(1,128)}, u32[]{:S(2)}) %copy-start.3) | copy-done | bytes 52
  7.6 0.7 %fusion.139 = (s32[1,1]{1,0:T(1,128)}, s32[1,1]{1,0:T(1,128)}, s32[1,1]{1,0:T(1,128)}, s32[1,1]{1,0:T(1,128)}, s32[1,1]{1,0:T(1,128)}, /*index=5*/s32[1,1]{1,0:T(1,128)}, s32[1,1]{1,0:T(1,128)}) fusion(s32[1,7]{1,0:T(1,128)S(1)} %and_select_fusion), kind=kLoop, calls=%fused_computation.175 | loop fusion | bytes 56 | tf_op jit(solution)/shard_map/slice | solution.py:41
  21.6 0.8 %copy-done.2 = f32[128,128]{1,0:T(8,128)S(1)} copy-done((f32[128,128]{1,0:T(8,128)S(1)}, f32[128,128]{1,0:T(8,128)}, u32[]{:S(2)}) %copy-start.2) | copy-done | bytes 65560
  22.8 0.2 convolution_add_fusion.11
  23.0 0.2 convolution_add_fusion.10
  23.2 0.2 convolution_add_fusion.9
  23.5 0.2 convolution_add_fusion.8
  23.7 0.2 convolution_add_fusion.7
  23.9 0.2 convolution_add_fusion.6
  24.1 7.2 %all_to_all.42 = f32[4,32,128]{2,1,0:T(8,128)} all-to-all(f32[4,32,128]{2,1,0:T(8,128)S(1)} %bitcast.176), channel_id=1, replica_groups=mesh['groups'=2,'rows'=4,'cols'=4] {'cols'}, dimensions={0} | all-to-all | bytes 131072 | tf_op jit(solution)/shard_map/all_to_all | solution.py:53
  31.3 4.1 %all-to-all-start.1 = ((f32[32,4,128]{2,0,1:T(8,128)}), f32[32,4,128]{2,0,1:T(8,128)}, u32[]{:S(2)}, u32[]{:S(2)}) async-start(f32[32,4,128]{2,0,1:T(8,128)} %bitcast.39), calls=%async_computation.1 | async-start | bytes 131072 | tf_op jit(solution)/shard_map/all_to_all | solution.py:55
  35.6 5.6 %all-to-all-done.1 = f32[32,4,128]{2,0,1:T(8,128)} async-done(((f32[32,4,128]{2,0,1:T(8,128)}), f32[32,4,128]{2,0,1:T(8,128)}, u32[]{:S(2)}, u32[]{:S(2)}) %all-to-all-start.1) | async-done | bytes 65568 | tf_op jit(solution)/shard_map/all_to_all | solution.py:55
  41.2 3.3 %all-to-all-start.2 = ((f32[4,32,128]{2,1,0:T(8,128)}), f32[4,32,128]{2,1,0:T(8,128)S(1)}, u32[]{:S(2)}, u32[]{:S(2)}) async-start(f32[4,32,128]{2,1,0:T(8,128)} %bitcast.40), calls=%async_computation.2 | async-start | bytes 131072 | tf_op jit(solution)/shard_map/all_to_all | solution.py:54
  45.2 3.4 %all-to-all-done.2 = f32[4,32,128]{2,1,0:T(8,128)S(1)} async-done(((f32[4,32,128]{2,1,0:T(8,128)}), f32[4,32,128]{2,1,0:T(8,128)S(1)}, u32[]{:S(2)}, u32[]{:S(2)}) %all-to-all-start.2) | async-done | bytes 65568 | tf_op jit(solution)/shard_map/all_to_all | solution.py:54
  48.6 0.7 %fusion.2 = f32[1,128,128]{2,0,1:T(1,128)S(1)} fusion(f32[1,8,128,128]{3,2,1,0:T(8,128)S(1)} %fusion.5, s32[]{:T(128)} %bitcast.156), kind=kOutput, calls=%fused_computation.15 | convolution fusion | flops 1572872 | bytes 589828 | tf_op jit(solution)/shard_map/dot_general | solution.py:76
  49.4 1.0 %collective-permute-start.5 = (f32[128,128]{0,1:T(8,128)S(1)}, f32[128,128]{0,1:T(8,128)S(1)}, u32[]{:S(2)}, u32[]{:S(2)}) collective-permute-start(f32[128,128]{0,1:T(8,128)S(1)} %bitcast.172), channel_id=1, source_target_pairs={{0,12},{4,0},{8,4},{12,8},{1,13},{5,1},{9,5},{13,9},{2,14},{6,2},{... | collective-permute-start | bytes 196616 | tf_op jit(solution)/shard_map/ppermute | solution.py:11
  50.4 1.4 %collective-permute-start.6 = (f32[128,128]{0,1:T(8,128)S(1)}, f32[128,128]{0,1:T(8,128)S(1)}, u32[]{:S(2)}, u32[]{:S(2)}) collective-permute-start(f32[128,128]{0,1:T(8,128)S(1)} %bitcast.173), channel_id=1, source_target_pairs={{0,8},{4,12},{8,0},{12,4},{1,9},{5,13},{9,1},{13,5},{2,10},{6,14},... | collective-permute-start | bytes 196616 | tf_op jit(solution)/shard_map/ppermute | solution.py:11
  51.8 0.4 collective-permute-start.7
  52.2 1.8 %collective-permute-done.5 = f32[128,128]{0,1:T(8,128)S(1)} collective-permute-done((f32[128,128]{0,1:T(8,128)S(1)}, f32[128,128]{0,1:T(8,128)S(1)}, u32[]{:S(2)}, u32[]{:S(2)}) %collective-permute-start.5) | collective-permute-done | bytes 65568 | tf_op jit(solution)/shard_map/ppermute | solution.py:11
  54.0 4.1 %collective-permute-done.6 = f32[128,128]{0,1:T(8,128)S(1)} collective-permute-done((f32[128,128]{0,1:T(8,128)S(1)}, f32[128,128]{0,1:T(8,128)S(1)}, u32[]{:S(2)}, u32[]{:S(2)}) %collective-permute-start.6) | collective-permute-done | bytes 65568 | tf_op jit(solution)/shard_map/ppermute | solution.py:11
  58.3 0.2 copy.11
  58.5 0.3 fusion.12
  58.8 0.3 convolution_add_fusion.5
  59.1 0.3 convolution_add_fusion.4
  59.4 0.3 convolution_add_fusion.3
  59.7 0.3 convolution_add_fusion.2
  60.0 0.3 convolution_add_fusion.1
  60.3 0.3 fusion.1
  60.6 0.7 %copy.13 = f32[128,128]{1,0:T(8,128)} copy(f32[128,128]{0,1:T(8,128)S(1)} %fusion.1) | data formatting | bytes 131072 | tf_op jit(solution)/shard_map/add | solution.py:98
  (37 shorter events, 0.9 us)
Async XLA Ops:
  0.0 21.5 %collective-permute-start = (f32[128,128]{1,0:T(8,128)}, f32[128,128]{1,0:T(8,128)S(1)}, u32[]{:S(2)}, u32[]{:S(2)}) collective-permute-start(f32[128,128]{1,0:T(8,128)} %param.7), channel_id=1, source_target_pairs={{0,0},{4,4},{8,8},{12,12},{1,1},{5,5},{9,9},{13,13},{2,2},{6,6},{1... | collective-permute-start | bytes 196616 | tf_op jit(solution)/shard_map/ppermute | solution.py:11
  0.8 20.7 %collective-permute-start.1 = (f32[128,128]{1,0:T(8,128)}, f32[128,128]{1,0:T(8,128)S(1)}, u32[]{:S(2)}, u32[]{:S(2)}) collective-permute-start(f32[128,128]{1,0:T(8,128)} %param.7), channel_id=1, source_target_pairs={{0,12},{4,0},{8,4},{12,8},{1,13},{5,1},{9,5},{13,9},{2,14},{6,2},{... | collective-permute-start | bytes 196616 | tf_op jit(solution)/shard_map/ppermute | solution.py:11
  5.9 15.7 %collective-permute-start.2 = (f32[128,128]{1,0:T(8,128)}, f32[128,128]{1,0:T(8,128)S(1)}, u32[]{:S(2)}, u32[]{:S(2)}) collective-permute-start(f32[128,128]{1,0:T(8,128)} %param.7), channel_id=1, source_target_pairs={{0,8},{4,12},{8,0},{12,4},{1,9},{5,13},{9,1},{13,5},{2,10},{6,14},... | collective-permute-start | bytes 196616 | tf_op jit(solution)/shard_map/ppermute | solution.py:11
  5.9 15.7 %collective-permute-start.3 = (f32[128,128]{1,0:T(8,128)}, f32[128,128]{1,0:T(8,128)S(1)}, u32[]{:S(2)}, u32[]{:S(2)}) collective-permute-start(f32[128,128]{1,0:T(8,128)} %param.7), channel_id=1, source_target_pairs={{0,4},{4,8},{8,12},{12,0},{1,5},{5,9},{9,13},{13,1},{2,6},{6,10},{... | collective-permute-start | bytes 196616 | tf_op jit(solution)/shard_map/ppermute | solution.py:11
  6.9 0.7 %copy-start.3 = (s32[1,7]{1,0:T(1,128)S(1)}, s32[1,7]{1,0:T(1,128)}, u32[]{:S(2)}) copy-start(s32[1,7]{1,0:T(1,128)} %param.8) | copy-start | bytes 88
  21.5 0.8 %copy-start.2 = (f32[128,128]{1,0:T(8,128)S(1)}, f32[128,128]{1,0:T(8,128)}, u32[]{:S(2)}) copy-start(f32[128,128]{1,0:T(8,128)} %param.7) | copy-start | bytes 196612
  21.5 1.0 %copy-start.1 = (f32[1,7,128,128]{3,2,1,0:T(8,128)S(1)}, f32[1,7,128,128]{3,2,1,0:T(8,128)}, u32[]{:S(2)}) copy-start(f32[1,7,128,128]{3,2,1,0:T(8,128)} %param.9) | copy-start | bytes 1376260
  23.4 11.9 %copy-start = (f32[8,128,128]{2,1,0:T(8,128)S(1)}, f32[8,128,128]{2,1,0:T(8,128)}, u32[]{:S(2)}) copy-start(f32[8,128,128]{2,1,0:T(8,128)} %param.11) | copy-start | bytes 1572868
  31.3 9.9 %all-to-all-start.1 = ((f32[32,4,128]{2,0,1:T(8,128)}), f32[32,4,128]{2,0,1:T(8,128)}, u32[]{:S(2)}, u32[]{:S(2)}) async-start(f32[32,4,128]{2,0,1:T(8,128)} %bitcast.39), calls=%async_computation.1 | async-start | bytes 131072 | tf_op jit(solution)/shard_map/all_to_all | solution.py:55
  41.2 7.4 %all-to-all-start.2 = ((f32[4,32,128]{2,1,0:T(8,128)}), f32[4,32,128]{2,1,0:T(8,128)S(1)}, u32[]{:S(2)}, u32[]{:S(2)}) async-start(f32[4,32,128]{2,1,0:T(8,128)} %bitcast.40), calls=%async_computation.2 | async-start | bytes 131072 | tf_op jit(solution)/shard_map/all_to_all | solution.py:54
  48.6 3.6 %collective-permute-start.4 = (f32[128,128]{0,1:T(8,128)S(1)}, f32[128,128]{0,1:T(8,128)S(1)}, u32[]{:S(2)}, u32[]{:S(2)}) collective-permute-start(f32[128,128]{0,1:T(8,128)S(1)} %bitcast.171), channel_id=1, source_target_pairs={{0,0},{4,4},{8,8},{12,12},{1,1},{5,5},{9,9},{13,13},{2,2},{6,6},{1... | collective-permute-start | bytes 196616 | tf_op jit(solution)/shard_map/ppermute | solution.py:11
  49.4 4.7 %collective-permute-start.5 = (f32[128,128]{0,1:T(8,128)S(1)}, f32[128,128]{0,1:T(8,128)S(1)}, u32[]{:S(2)}, u32[]{:S(2)}) collective-permute-start(f32[128,128]{0,1:T(8,128)S(1)} %bitcast.172), channel_id=1, source_target_pairs={{0,12},{4,0},{8,4},{12,8},{1,13},{5,1},{9,5},{13,9},{2,14},{6,2},{... | collective-permute-start | bytes 196616 | tf_op jit(solution)/shard_map/ppermute | solution.py:11
  50.4 7.8 %collective-permute-start.6 = (f32[128,128]{0,1:T(8,128)S(1)}, f32[128,128]{0,1:T(8,128)S(1)}, u32[]{:S(2)}, u32[]{:S(2)}) collective-permute-start(f32[128,128]{0,1:T(8,128)S(1)} %bitcast.173), channel_id=1, source_target_pairs={{0,8},{4,12},{8,0},{12,4},{1,9},{5,13},{9,1},{13,5},{2,10},{6,14},... | collective-permute-start | bytes 196616 | tf_op jit(solution)/shard_map/ppermute | solution.py:11
  51.8 6.4 %collective-permute-start.7 = (f32[128,128]{0,1:T(8,128)S(1)}, f32[128,128]{0,1:T(8,128)S(1)}, u32[]{:S(2)}, u32[]{:S(2)}) collective-permute-start(f32[128,128]{0,1:T(8,128)S(1)} %bitcast.174), channel_id=1, source_target_pairs={{0,4},{4,8},{8,12},{12,0},{1,5},{5,9},{9,13},{13,1},{2,6},{6,10},{... | collective-permute-start | bytes 196616 | tf_op jit(solution)/shard_map/ppermute | solution.py:11
where the time goes:
time: 61.9 us; the launch traced here: 61.3 us
  starting transfers between devices  17.1 us (28%)
  waiting for transfers between devices  15 us (24%)
  between operations  14.2 us (23%)
  blocking collectives  7.16 us (12%)
  matrix products  4.21 us (7%)
  local copies, waits for them, and re-layouts  3.63 us (6%)
    ppermute x8, starting transfers between devices, passed_along(): lax.ppermute(value, axis, [(i, (i + by) % size) for i in range(size)])  9.73 us
    all_to_all x1, blocking collectives, transpose_tile(): lax.all_to_all(local_tile, 'cols', split_axis=0, concat_axis=1, tiled=True)  7.16 us
    ppermute x8, waiting for transfers between devices, passed_along(): lax.ppermute(value, axis, [(i, (i + by) % size) for i in range(size)])  5.97 us
    all_to_all x1, waiting for transfers between devices, transpose_tile(): lax.all_to_all(section_one, 'rows', split_axis=1, concat_axis=0, tiled=True)  5.64 us
    all_to_all x1, starting transfers between devices, transpose_tile(): lax.all_to_all(section_one, 'rows', split_axis=1, concat_axis=0, tiled=True)  4.08 us
    dot_general x14, matrix products, propagate_rows(): jnp.einsum('iab,ibw->iaw', trans_blocks[:, column_slot], picked, precisio...  3.56 us
    all_to_all x1, waiting for transfers between devices, transpose_tile(): lax.all_to_all(lax.all_to_all(section_one, 'rows', split_axis=1, concat_a...  3.37 us
    all_to_all x1, starting transfers between devices, transpose_tile(): lax.all_to_all(lax.all_to_all(section_one, 'rows', split_axis=1, concat_a...  3.28 us
  transfers between devices with their start and end apart: 10, of which 4 were waited for; matrix products, arithmetic and copies ran while one was open for 3% of the time, Pallas kernels for 0%

commit v1 on v0

--- a/solution.py
+++ b/solution.py
@@ -1,9 +1,14 @@
+import functools
+
 import jax
 import jax.numpy as jnp
 from jax import lax
+from jax.experimental import pallas as pl
+from jax.experimental.pallas import tpu as pltpu
 from jax.sharding import PartitionSpec as P
 
 REACH = 4
+MESH = pl.DeviceIdType.MESH
 
 
 def passed_along(value, axis, by):
@@ -91,11 +96,227 @@
     return present * placed
 
 
+def split(value):
+    high = value.astype(jnp.bfloat16)
+    return high, (value - high.astype(jnp.float32)).astype(jnp.bfloat16)
+
+
+def product(left, right):
+    left_high, left_low = left
+    right_high, right_low = right
+    dot = functools.partial(jnp.dot, preferred_element_type=jnp.float32)
+    return dot(left_high, right_high) + (dot(left_high, right_low) + dot(left_low, right_high))
+
+
+def square_kernel(
+    size,
+    cols_ref,
+    pattern_ref,
+    cov_ref,
+    trans_ref,
+    table_ref,
+    out_ref,
+    trans,
+    table,
+    own,
+    rows_high,
+    rows_low,
+    turned_high,
+    turned_low,
+    tiles,
+    sending,
+    pieces,
+    noise,
+    local_sem,
+    tile_send,
+    tile_recv,
+    piece_send,
+    piece_recv,
+):
+    group = lax.axis_index("groups")
+    row = lax.axis_index("rows")
+    col = lax.axis_index("cols")
+    diagonal = row == col
+
+    get_cov = pltpu.make_async_copy(cov_ref, own, local_sem.at[0])
+    get_trans = pltpu.make_async_copy(trans_ref, trans, local_sem.at[1])
+    get_table = pltpu.make_async_copy(table_ref, table, local_sem.at[2])
+    get_cov.start()
+    get_trans.start()
+    get_table.start()
+
+    barrier = pltpu.get_barrier_semaphore()
+
+    def greet(to_row, to_col):
+        pl.semaphore_signal(
+            barrier, inc=1, device_id=(group, to_row, to_col), device_id_type=MESH
+        )
+
+    for step in range(1, size):
+        greet((row + step) % size, col)
+        greet(col, (row + step) % size)
+
+    @pl.when(jnp.logical_not(diagonal))
+    def _():
+        greet(col, row)
+
+    get_cov.wait()
+    sending[...] = own[...].T
+    get_trans.wait()
+    for j in range(size):
+        block = jnp.zeros(own.shape, jnp.float32)
+        for k in range(trans.shape[1]):
+            block = block + jnp.where(cols_ref[0, k] == j, trans[0, k], 0.0)
+        high, low = split(block)
+        rows_high[j] = high
+        rows_low[j] = low
+        high, low = split(block.T)
+        turned_high[j] = high
+        turned_low[j] = low
+    get_table.wait()
+    noise[...] = jnp.zeros(noise.shape, jnp.float32)
+
+    @pl.when(diagonal)
+    def _():
+        kind = table[pattern_ref[0]]
+        noise[...] = (kind + kind.T) * 0.5
+
+    @pl.when(diagonal)
+    def _():
+        pl.semaphore_wait(barrier, 2 * (size - 1))
+
+    @pl.when(jnp.logical_not(diagonal))
+    def _():
+        pl.semaphore_wait(barrier, 2 * size - 1)
+
+    tile_copies = []
+    for step in range(1, size):
+        tile_copies.append(
+            pltpu.make_async_remote_copy(
+                src_ref=sending,
+                dst_ref=tiles.at[step - 1],
+                send_sem=tile_send.at[step - 1],
+                recv_sem=tile_recv.at[step - 1],
+                device_id=(group, (row + step) % size, col),
+                device_id_type=MESH,
+            )
+        )
+        tile_copies[-1].start()
+
+    total = product(split(sending[...]), (turned_high[row], turned_low[row]))
+    for step in range(1, size):
+        tile_copies[step - 1].wait_recv()
+        source = (row + size - step) % size
+        total = total + product(
+            split(tiles[step - 1]), (turned_high[source], turned_low[source])
+        )
+    for copy in tile_copies:
+        copy.wait_send()
+    sending[...] = total
+
+    def piece_copy(step):
+        return pltpu.make_async_remote_copy(
+            src_ref=sending,
+            dst_ref=pieces.at[col],
+            send_sem=piece_send.at[step],
+            recv_sem=piece_recv.at[col],
+            device_id=(group, (row + step) % size, row),
+            device_id_type=MESH,
+        )
+
+    def arrival(source):
+        return pltpu.make_async_remote_copy(
+            src_ref=sending,
+            dst_ref=pieces.at[source],
+            send_sem=piece_send.at[0],
+            recv_sem=piece_recv.at[source],
+            device_id=(group, col, source),
+            device_id_type=MESH,
+        )
+
+    for step in range(1, size):
+        piece_copy(step).start()
+
+    @pl.when(jnp.logical_not(diagonal))
+    def _():
+        piece_copy(0).start()
+
+    @pl.when(diagonal)
+    def _():
+        pieces[col] = sending[...]
+
+    result = noise[...]
+    for step in range(size):
+        source = (col + step) % size
+        if step == 0:
+
+            @pl.when(jnp.logical_not(diagonal))
+            def _():
+                arrival(source).wait_recv()
+        else:
+            arrival(source).wait_recv()
+        result = result + product(
+            (rows_high[source], rows_low[source]), split(pieces[source])
+        )
+    out_ref[...] = result
+
+    for step in range(1, size):
+        piece_copy(step).wait_send()
+
+    @pl.when(jnp.logical_not(diagonal))
+    def _():
+        piece_copy(0).wait_send()
+
+
+def square_body(covariance, block_cols, trans_blocks, noise_pattern, noise_table):
+    size = lax.axis_size("rows")
+    tile = covariance.shape
+    copies = pltpu.SemaphoreType.DMA
+    return pl.pallas_call(
+        functools.partial(square_kernel, size),
+        out_shape=jax.ShapeDtypeStruct(tile, jnp.float32),
+        in_specs=[
+            pl.BlockSpec(memory_space=pltpu.SMEM),
+            pl.BlockSpec(memory_space=pltpu.SMEM),
+            pl.BlockSpec(memory_space=pl.ANY),
+            pl.BlockSpec(memory_space=pl.ANY),
+            pl.BlockSpec(memory_space=pl.ANY),
+        ],
+        out_specs=pl.BlockSpec(memory_space=pltpu.VMEM),
+        scratch_shapes=[
+            pltpu.VMEM(trans_blocks.shape, jnp.float32),
+            pltpu.VMEM(noise_table.shape, jnp.float32),
+            pltpu.VMEM(tile, jnp.float32),
+            pltpu.VMEM((size, *tile), jnp.bfloat16),
+            pltpu.VMEM((size, *tile), jnp.bfloat16),
+            pltpu.VMEM((size, *tile), jnp.bfloat16),
+            pltpu.VMEM((size, *tile), jnp.bfloat16),
+            pltpu.VMEM((size - 1, *tile), jnp.float32),
+            pltpu.VMEM(tile, jnp.float32),
+            pltpu.VMEM((size, *tile), jnp.float32),
+            pltpu.VMEM(tile, jnp.float32),
+            copies((3,)),
+            copies((size - 1,)),
+            copies((size - 1,)),
+            copies((size,)),
+            copies((size,)),
+        ],
+        compiler_params=pltpu.CompilerParams(collective_id=0, has_side_effects=True),
+    )(block_cols, noise_pattern, covariance, trans_blocks, noise_table)
+
+
 def body(covariance, block_cols, trans_blocks, noise_pattern, noise_table):
     tile_height, tile_width = covariance.shape
     propagated = propagate_rows(covariance, block_cols, trans_blocks)
     carried = propagate_rows(transpose_tile(propagated), block_cols, trans_blocks)
     return carried + noise_tile(noise_pattern, noise_table, tile_height, tile_width)
+
+
+def device_body(covariance, block_cols, trans_blocks, noise_pattern, noise_table):
+    block = trans_blocks.shape[2]
+    square = lax.axis_size("rows") == lax.axis_size("cols")
+    chosen = square_body if square and covariance.shape == (block, block) else body
+    return chosen(covariance, block_cols, trans_blocks, noise_pattern, noise_table)
 
 
 def solution(mesh):
@@ -107,5 +328,5 @@
         P(),
     )
     return jax.shard_map(
-        body, mesh=mesh, in_specs=placed, out_specs=P(("groups", "rows"), "cols"), check_vma=False
-    )
+        device_body, mesh=mesh, in_specs=placed, out_specs=P(("groups", "rows"), "cols"), check_vma=False
+    )

time: 61.9 us -> 21.6 us (0.35)
  the two profiles are of different devices: /device:TPU:0 before, /device:TPU:1 now
where the time goes in v1:
time: 21.6 us; the launch traced here: 21.2 us
  Pallas kernels  19 us (88%)
  local copies, waits for them, and re-layouts  1.47 us (7%)
  between operations  0.66 us (3%)
    pallas_call x1, Pallas kernels, square_body(): pl.pallas_call(functools.partial(square_kernel, size), out_shape=jax.Shap...  19 us
    unnamed x1, local copies, waits for them, and re-layouts  1.47 us

profile of v1, /device:TPU:1, one launch (start us, length us, event | category | flops | bytes accessed | tf_op | source)
XLA Modules:
  0.0 21.2 jit_solution(2274815008442902271)
XLA Ops:
  0.7 19.0 %shard_map.55 = f32[128,128]{1,0:T(8,128)} custom-call(s32[1,7]{1,0:T(1,128)} %cols_ref.1, s32[1]{0:T(128)S(6)} %copy.7.pattern_ref, f32[128,128]{1,0:T(8,128)} %cov_ref.1, f32[1,7,128,128]{3,2,1,0:T(8,128)} %trans_ref.1, f32[8,128,128]{2,1,0:T(8,128)} %table_ref.1), custom_call_target="tpu_custom_call" | custom-call | tf_op jit(solution)/shard_map/pallas_call | solution.py:275
  19.7 1.5 %copy.8 = f32[128,128]{1,0:T(8,128)} copy(f32[128,128]{1,0:T(8,128)} %shard_map.55) | data formatting | bytes 131072

commit v2 on v1

--- a/solution.py
+++ b/solution.py
@@ -8,6 +8,7 @@
 from jax.sharding import PartitionSpec as P
 
 REACH = 4
+CHUNKS = 2
 MESH = pl.DeviceIdType.MESH
 
 
@@ -125,6 +126,7 @@
     turned_low,
     tiles,
     sending,
+    turned,
     pieces,
     noise,
     local_sem,
@@ -189,83 +191,90 @@
     def _():
         pl.semaphore_wait(barrier, 2 * size - 1)
 
-    tile_copies = []
-    for step in range(1, size):
-        tile_copies.append(
-            pltpu.make_async_remote_copy(
-                src_ref=sending,
-                dst_ref=tiles.at[step - 1],
-                send_sem=tile_send.at[step - 1],
-                recv_sem=tile_recv.at[step - 1],
-                device_id=(group, (row + step) % size, col),
-                device_id_type=MESH,
-            )
-        )
-        tile_copies[-1].start()
-
-    total = product(split(sending[...]), (turned_high[row], turned_low[row]))
-    for step in range(1, size):
-        tile_copies[step - 1].wait_recv()
-        source = (row + size - step) % size
-        total = total + product(
-            split(tiles[step - 1]), (turned_high[source], turned_low[source])
-        )
-    for copy in tile_copies:
-        copy.wait_send()
-    sending[...] = total
-
-    def piece_copy(step):
+    depth = own.shape[0] // CHUNKS
+
+    def tile_copy(step, chunk):
+        rows = pl.ds(chunk * depth, depth)
         return pltpu.make_async_remote_copy(
-            src_ref=sending,
-            dst_ref=pieces.at[col],
-            send_sem=piece_send.at[step],
-            recv_sem=piece_recv.at[col],
+            src_ref=sending.at[rows],
+            dst_ref=tiles.at[step - 1, rows],
+            send_sem=tile_send.at[step - 1, chunk],
+            recv_sem=tile_recv.at[step - 1, chunk],
+            device_id=(group, (row + step) % size, col),
+            device_id_type=MESH,
+        )
+
+    def piece_copy(step, chunk):
+        rows = pl.ds(chunk * depth, depth)
+        return pltpu.make_async_remote_copy(
+            src_ref=turned.at[rows],
+            dst_ref=pieces.at[col, rows],
+            send_sem=piece_send.at[step, chunk],
+            recv_sem=piece_recv.at[col, chunk],
             device_id=(group, (row + step) % size, row),
             device_id_type=MESH,
         )
 
-    def arrival(source):
+    def arrival(source, chunk):
+        rows = pl.ds(chunk * depth, depth)
         return pltpu.make_async_remote_copy(
-            src_ref=sending,
-            dst_ref=pieces.at[source],
-            send_sem=piece_send.at[0],
-            recv_sem=piece_recv.at[source],
+            src_ref=turned.at[rows],
+            dst_ref=pieces.at[source, rows],
+            send_sem=piece_send.at[0, chunk],
+            recv_sem=piece_recv.at[source, chunk],
             device_id=(group, col, source),
             device_id_type=MESH,
         )
 
-    for step in range(1, size):
-        piece_copy(step).start()
-
-    @pl.when(jnp.logical_not(diagonal))
-    def _():
-        piece_copy(0).start()
+    for chunk in range(CHUNKS):
+        for step in range(1, size):
+            tile_copy(step, chunk).start()
+
+    for chunk in range(CHUNKS):
+        rows = pl.ds(chunk * depth, depth)
+        total = product(split(sending[rows]), (turned_high[row], turned_low[row]))
+        for step in range(1, size):
+            tile_copy(step, chunk).wait_recv()
+            source = (row + size - step) % size
+            total = total + product(
+                split(tiles[step - 1, rows]), (turned_high[source], turned_low[source])
+            )
+        turned[rows] = total
+        for step in range(1, size):
+            piece_copy(step, chunk).start()
+
+        @pl.when(jnp.logical_not(diagonal))
+        def _():
+            piece_copy(0, chunk).start()
 
     @pl.when(diagonal)
     def _():
-        pieces[col] = sending[...]
+        pieces[col] = turned[...]
 
     result = noise[...]
     for step in range(size):
         source = (col + step) % size
-        if step == 0:
-
-            @pl.when(jnp.logical_not(diagonal))
-            def _():
-                arrival(source).wait_recv()
-        else:
-            arrival(source).wait_recv()
+        for chunk in range(CHUNKS):
+            if step == 0:
+
+                @pl.when(jnp.logical_not(diagonal))
+                def _():
+                    arrival(source, chunk).wait_recv()
+            else:
+                arrival(source, chunk).wait_recv()
         result = result + product(
             (rows_high[source], rows_low[source]), split(pieces[source])
         )
     out_ref[...] = result
 
-    for step in range(1, size):
-        piece_copy(step).wait_send()
-
-    @pl.when(jnp.logical_not(diagonal))
-    def _():
-        piece_copy(0).wait_send()
+    for chunk in range(CHUNKS):
+        for step in range(1, size):
+            tile_copy(step, chunk).wait_send()
+            piece_copy(step, chunk).wait_send()
+
+        @pl.when(jnp.logical_not(diagonal))
+        def _():
+            piece_copy(0, chunk).wait_send()
 
 
 def square_body(covariance, block_cols, trans_blocks, noise_pattern, noise_table):
@@ -293,13 +302,14 @@
             pltpu.VMEM((size, *tile), jnp.bfloat16),
             pltpu.VMEM((size - 1, *tile), jnp.float32),
             pltpu.VMEM(tile, jnp.float32),
+            pltpu.VMEM(tile, jnp.float32),
             pltpu.VMEM((size, *tile), jnp.float32),
             pltpu.VMEM(tile, jnp.float32),
             copies((3,)),
-            copies((size - 1,)),
-            copies((size - 1,)),
-            copies((size,)),
-            copies((size,)),
+            copies((size - 1, CHUNKS)),
+            copies((size - 1, CHUNKS)),
+            copies((size, CHUNKS)),
+            copies((size, CHUNKS)),
         ],
         compiler_params=pltpu.CompilerParams(collective_id=0, has_side_effects=True),
     )(block_cols, noise_pattern, covariance, trans_blocks, noise_table)

time: 21.6 us -> 20.8 us (0.963)
  Pallas kernels: 19 us -> 18.4 us
    pallas_call x1, Pallas kernels: 19 us -> 18.4 us  [square_body(): pl.pallas_call(functools.partial(square_kernel, size), out_shape=jax.Shap...]
where the time goes in v2:
time: 20.8 us; the launch traced here: 20.6 us
  Pallas kernels  18.4 us (88%)
  local copies, waits for them, and re-layouts  1.47 us (7%)
  between operations  0.66 us (3%)
    pallas_call x1, Pallas kernels, square_body(): pl.pallas_call(functools.partial(square_kernel, size), out_shape=jax.Shap...  18.4 us
    unnamed x1, local copies, waits for them, and re-layouts  1.47 us

profile of v2, /device:TPU:1, one launch (start us, length us, event | category | flops | bytes accessed | tf_op | source)
XLA Modules:
  0.0 20.6 jit_solution(3704550340279271973)
XLA Ops:
  0.7 18.4 %shard_map.55 = f32[128,128]{1,0:T(8,128)} custom-call(s32[1,7]{1,0:T(1,128)} %cols_ref.1, s32[1]{0:T(128)S(6)} %copy.7.pattern_ref, f32[128,128]{1,0:T(8,128)} %cov_ref.1, f32[1,7,128,128]{3,2,1,0:T(8,128)} %trans_ref.1, f32[8,128,128]{2,1,0:T(8,128)} %table_ref.1), custom_call_target="tpu_custom_call" | custom-call | tf_op jit(solution)/shard_map/pallas_call | solution.py:284
  19.1 1.5 %copy.8 = f32[128,128]{1,0:T(8,128)} copy(f32[128,128]{1,0:T(8,128)} %shard_map.55) | data formatting | bytes 131072
